TPU v7x, 256 devices: a whole 4x4x8 slice. The times are simulated.
256 devices in a mesh: gx: 8 (over y, core), gy: 32 (over x, z).
Axes of the slice: x: 4, y: 4, z: 8, core: 2. Of those that a mesh axis runs over, the one named last changes fastest.
Arguments:
- query: bfloat16 [192, 4, 64, 128], P(None, None, 'gx'), may hold values from -10 to 10
- cache_key: bfloat16 [192, 8, 2048, 128], P('gy', 'gx'), may hold values from -10 to 10
- cache_value: bfloat16 [192, 8, 2048, 128], P('gy', 'gx'), may hold values from -18 to 18
- new_key: bfloat16 [192, 4, 8, 128], P('gy', None, 'gx'), may hold values from -10 to 10
- new_value: bfloat16 [192, 4, 8, 128], P('gy', None, 'gx'), may hold values from -18 to 18
- prefix_len: int32 [192], replicated, may hold values from 1 to 2048, as said below
- residual: bfloat16 [768, 8192], P('gx', 'gy'), may hold values from -1.796875 to 1.796875
- out_weight: bfloat16 [8192, 8192], P('gx', 'gy'), may hold values from -0.0625 to 0.0625
- norm_gain: float32 [8192], replicated, may hold values from 0.1 to 1.9
- gate_weight: bfloat16 [8192, 28672], P('gx', 'gy'), may hold values from -0.0625 to 0.0625
- up_weight: bfloat16 [8192, 28672], P('gx', 'gy'), may hold values from -0.0625 to 0.0625
Outputs:
- stream: bfloat16 [768, 8192], P('gx', 'gy')
- activated: bfloat16 [768, 28672], P('gx', 'gy')
Inputs may be any that keep to these rules, and one draw needn't show every extreme that they name: `prefix_len`: one rollout's prefix holds exactly 2048 live slots and another's exactly 1.
All inputs are finite; a program needn't handle non-finite values.
Results may differ from a plain program's by a relative error of at most 0.04.
Values may be sent and summed in bfloat16 or wider, within the bound.
A program may use at most 128 MiB of HBM per device.

v0:
```python
import jax
import jax.numpy as jnp
from jax import lax
from jax.sharding import PartitionSpec as P

masked_score = -1e30
norm_eps = 1e-05


def fresh_part(queries, new_key, new_value, scale):
    count = queries.shape[1]
    scores = (
        jnp.einsum("rtkgd,rskd->rkgts", queries, new_key, preferred_element_type=jnp.float32)
        * scale
    )
    causal = jnp.arange(count)[None, :] <= jnp.arange(count)[:, None]
    scores = jnp.where(causal, scores, masked_score)
    top = scores.max(-1)
    weights = jnp.where(causal, jnp.exp(scores - top[..., None]), 0.0)
    mixed = jnp.einsum(
        "rkgts,rskd->rkgtd",
        weights.astype(jnp.bfloat16),
        new_value,
        preferred_element_type=jnp.float32,
    )
    return (top, weights.sum(-1), mixed)


def cache_part(queries, keys, values, places, lengths, scale):
    scores = (
        jnp.einsum("rtkgd,rkpd->rkgtp", queries, keys, preferred_element_type=jnp.float32) * scale
    )
    valid = (places[None, :] < lengths[:, None])[:, None, None, None, :]
    scores = jnp.where(valid, scores, masked_score)
    top = scores.max(-1)
    weights = jnp.where(valid, jnp.exp(scores - top[..., None]), 0.0)
    mixed = jnp.einsum(
        "rkgtp,rkpd->rkgtd",
        weights.astype(jnp.bfloat16),
        values,
        preferred_element_type=jnp.float32,
    )
    return (top, weights.sum(-1), mixed)


def walk_blocks(queries, keys, values, lengths, steps_needed, block_len, stride, scale):
    rows, count, kv_local, group_size, head_size = queries.shape

    def visit(block, carry):
        run_top, run_total, run_mixed = carry
        key_block = lax.dynamic_slice_in_dim(keys, block * block_len, block_len, 2)
        value_block = lax.dynamic_slice_in_dim(values, block * block_len, block_len, 2)
        places = (block * block_len + jnp.arange(block_len, dtype=jnp.int32)) * stride
        blk_top, blk_total, blk_mixed = cache_part(
            queries, key_block, value_block, places, lengths, scale
        )
        merged = jnp.maximum(run_top, blk_top)
        old_scale = jnp.exp(run_top - merged)
        blk_scale = jnp.exp(blk_top - merged)
        run_total = run_total * old_scale + blk_total * blk_scale
        run_mixed = run_mixed * old_scale[..., None] + blk_mixed * blk_scale[..., None]
        return (merged, run_total, run_mixed)

    start_top = jnp.full((rows, kv_local, group_size, count), masked_score, jnp.float32)
    start_total = jnp.zeros((rows, kv_local, group_size, count), jnp.float32)
    start_mixed = jnp.zeros((rows, kv_local, group_size, count, head_size), jnp.float32)
    return lax.fori_loop(0, steps_needed, visit, (start_top, start_total, start_mixed))


def combine(part_top, part_total, part_mixed, new_top, new_total, new_mixed):
    top = jnp.maximum(new_top, part_top.max(0))
    new_scale = jnp.exp(new_top - top)
    part_scale = jnp.exp(part_top - top)
    total = new_total * new_scale + (part_total * part_scale).sum(0)
    mixed = new_mixed * new_scale[..., None] + (part_mixed * part_scale[..., None]).sum(0)
    return mixed / total[..., None]


def on_device(
    query,
    cache_key,
    cache_value,
    new_key,
    new_value,
    prefix_len,
    residual,
    out_weight,
    norm_gain,
    gate_weight,
    up_weight,
):
    roll_local = cache_key.shape[0]
    kv_local = cache_key.shape[1]
    new_count = query.shape[1]
    head_size = query.shape[3]
    group_size = query.shape[2] // kv_local
    cache_len = cache_key.shape[2]
    scale = head_size ** (-0.5)
    my_index = lax.axis_index("gy")
    own_query = lax.dynamic_slice_in_dim(query, my_index * roll_local, roll_local, 0)
    own_query = own_query.reshape(roll_local, new_count, kv_local, group_size, head_size)
    new_top, new_total, new_mixed = fresh_part(own_query, new_key, new_value, scale)
    own_len = lax.dynamic_slice_in_dim(prefix_len, my_index * roll_local, roll_local, 0)
    block_len = min(512, cache_len)
    steps_needed = (own_len.max() + block_len - 1) // block_len
    run_top, run_total, run_mixed = walk_blocks(
        own_query, cache_key, cache_value, own_len, steps_needed, block_len, 1, scale
    )
    heads = combine(run_top[None], run_total[None], run_mixed[None], new_top, new_total, new_mixed)
    head_rows = (
        heads.transpose(0, 3, 1, 2, 4)
        .reshape(roll_local * new_count, kv_local * group_size * head_size)
        .astype(jnp.bfloat16)
    )
    partial_proj = jnp.dot(
        lax.all_gather(head_rows, "gy", axis=0, tiled=True),
        out_weight,
        preferred_element_type=jnp.float32,
    )
    summed = lax.psum_scatter(
        partial_proj.astype(jnp.bfloat16), "gx", scatter_dimension=0, tiled=True
    ).astype(jnp.float32)
    stream = (residual.astype(jnp.float32) + summed).astype(jnp.bfloat16)
    full_rows = lax.all_gather(stream, "gy", axis=1, tiled=True).astype(jnp.float32)
    normed = (
        full_rows
        * lax.rsqrt(jnp.mean(full_rows * full_rows, axis=-1, keepdims=True) + norm_eps)
        * norm_gain
    ).astype(jnp.bfloat16)
    feature_rows = lax.all_to_all(normed, "gx", split_axis=1, concat_axis=0, tiled=True)
    hidden_local = gate_weight.shape[1]
    gate = jnp.dot(feature_rows, gate_weight, preferred_element_type=jnp.float32)
    up = jnp.dot(feature_rows, up_weight, preferred_element_type=jnp.float32)
    both = lax.psum_scatter(
        jnp.concatenate([gate, up], axis=1).astype(jnp.bfloat16),
        "gx",
        scatter_dimension=0,
        tiled=True,
    ).astype(jnp.float32)
    activated = (jax.nn.silu(both[:, :hidden_local]) * both[:, hidden_local:]).astype(jnp.bfloat16)
    return (stream, activated)


def solution(mesh):
    in_specs = (
        P(None, None, "gx", None),
        P("gy", "gx", None, None),
        P("gy", "gx", None, None),
        P("gy", None, "gx", None),
        P("gy", None, "gx", None),
        P(),
        P("gx", "gy"),
        P("gx", "gy"),
        P(),
        P("gx", "gy"),
        P("gx", "gy"),
    )
    out_specs = (P("gx", "gy"), P("gx", "gy"))
    return jax.shard_map(
        on_device, mesh=mesh, in_specs=in_specs, out_specs=out_specs, check_vma=False
    )
```

profile of v0, /device:TPU:1, one launch (start us, length us, event | category | flops | bytes accessed | tf_op | source)
XLA Modules:
  0.0 290.8 jit_solution(12733897574460884842)
XLA Ops:
  7.2 1.5 fusion.53
  9.4 0.8 dynamic-slice_bitcast_fusion
  10.3 13.8 %while.14 = (s32[]{:T(128)}, f32[6,1,8,4]{2,3,0,1:T(4,128)S(1)}, f32[6,1,8,4]{2,3,0,1:T(4,128)S(1)}, f32[6,1,8,4,128]{4,2,3,0,1:T(8,128)S(1)}, s32[]{:T(128)}, /...) while((s32[]{:T(128)}, f32[6,1,8,4]{2,3,0,1:T(4,128)S(1)}, ...), condition=%wide.region_5.6_spmd, body=%wide.region_2.5_spmd.sunk | while | flops 51294660 | bytes 3029455 | solution.py:67
  10.4 1.6 fusion.71
  12.0 0.2 fusion.73
  12.3 1.5 fusion.75
  13.9 1.6 fusion.71
  15.5 0.2 fusion.73
  15.8 1.5 fusion.75
  17.3 1.6 fusion.71
  18.9 0.2 fusion.73
  19.2 1.4 fusion.75
  20.8 1.6 fusion.71
  22.3 0.2 fusion.73
  22.6 1.5 fusion.75
  24.1 1.1 fusion.55
  25.5 0.3 fusion.29
  25.8 0.6 copy.27
  26.5 76.7 %all-gather.3.cloned.1.call-done = bf16[768,1024]{1,0:T(8,128)(2,1)} async-done(((bf16[24,1024]{1,0:T(8,128)(2,1)}), bf16[768,1024]{1,0:T(8,128)(2,1)}) %all-gather.3.cloned.1.call-update) | async-done | bytes 1572880 | tf_op jit(solution)/shard_map/all_gather | solution.py:116
  103.2 2.7 convolution_convert_fusion.2
  106.0 32.8 %reduce-scatter.3.cloned.1.call-done = bf16[96,256]{1,0:T(8,128)(2,1)} async-done(((bf16[768,256]{1,0:T(8,128)(2,1)}), bf16[96,256]{1,0:T(8,128)(2,1)}) %reduce-scatter.3.cloned.1.call-update) | async-done | bytes 49168 | tf_op jit(solution)/shard_map/reduce_scatter | solution.py:120
  138.8 1.4 add_convert_fusion
  140.3 72.5 %all-gather.5.cloned.1.call-done = bf16[96,8192]{1,0:T(8,128)(2,1)} async-done(((bf16[96,256]{1,0:T(8,128)(2,1)}), bf16[96,8192]{1,0:T(8,128)(2,1)}) %all-gather.5.cloned.1.call-update) | async-done | bytes 1572880 | tf_op jit(solution)/shard_map/all_gather | solution.py:124
  212.8 1.9 fusion.24
  214.8 0.5 fusion.26
  215.4 28.9 %all_to_all.19 = bf16[96,8,1024]{2,0,1:T(8,128)(2,1)S(1)} all-to-all(bf16[96,8,1024]{2,0,1:T(8,128)(2,1)S(1)} %bitcast.132), channel_id=1, replica_groups=mesh['gx'=8,'gy'=32] {'gx'}, dimensions={1} | all-to-all | bytes 3145728 | tf_op jit(solution)/shard_map/all_to_all | solution.py:130
  244.3 1.8 convolution_convert_fusion
  246.1 1.8 convolution_convert_fusion.1
  247.9 1.8 pad_maximum_fusion
  249.7 32.8 %reduce-scatter.5.cloned.1.call-done = bf16[96,1792]{1,0:T(8,128)(2,1)} async-done(((bf16[768,1792]{1,0:T(8,128)(2,1)}), bf16[96,1792]{1,0:T(8,128)(2,1)}) %reduce-scatter.5.cloned.1.call-update) | async-done | bytes 344080 | tf_op jit(solution)/shard_map/reduce_scatter | solution.py:134
  282.5 1.0 convert_element_type.54
  283.5 0.8 fusion.32
  (53 shorter events, 1.1 us)
Async XLA Ops:
  7.2 237.1 %copy-start = (bf16[1024,896]{1,0:T(8,128)(2,1)S(1)}, bf16[1024,896]{1,0:T(8,128)(2,1)}, u32[]{:S(2)}) copy-start(bf16[1024,896]{1,0:T(8,128)(2,1)} %param.23) | copy-start | bytes 5505028
  7.2 96.0 %all-gather.3.cloned.1.call-start = ((), (), s32[]{:S(2)}) async-start(), calls=%async_computation.3 | async-start | bytes 1622016 | tf_op jit(solution)/shard_map/all_gather | solution.py:116
  10.3 13.9 %copy-start.6 = (bf16[6,4,1,128]{3,1,2,0:T(4,128)(2,1)S(1)}, bf16[6,4,1,128]{3,1,2,0:T(4,128)(2,1)}, u32[]{:S(2)}) copy-start(bf16[6,4,1,128]{3,1,2,0:T(4,128)(2,1)} %param.16) | copy-start | bytes 18436
  10.3 15.2 %copy-start.7 = (bf16[6,4,1,128]{3,1,2,0:T(4,128)(2,1)S(1)}, bf16[6,4,1,128]{3,1,2,0:T(4,128)(2,1)}, u32[]{:S(2)}) copy-start(bf16[6,4,1,128]{3,1,2,0:T(4,128)(2,1)} %param.17) | copy-start | bytes 18436
  10.3 92.9 %copy-start.5 = (bf16[1024,256]{1,0:T(8,128)(2,1)S(1)}, bf16[1024,256]{1,0:T(8,128)(2,1)}, u32[]{:S(2)}) copy-start(bf16[1024,256]{1,0:T(8,128)(2,1)} %param.20) | copy-start | bytes 1572868
  25.7 113.1 %copy-start.2 = (bf16[96,256]{1,0:T(8,128)(2,1)S(1)}, bf16[96,256]{1,0:T(8,128)(2,1)}, u32[]{:S(2)}) copy-start(bf16[96,256]{1,0:T(8,128)(2,1)} %param.19) | copy-start | bytes 147460
  26.4 188.3 %copy-start.3 = (f32[8192]{0:T(1024)S(1)}, f32[8192]{0:T(1024)}, u32[]{:S(2)}) copy-start(f32[8192]{0:T(1024)} %param.21) | copy-start | bytes 98308
  26.4 112.4 %reduce-scatter.3.cloned.1.call-start = ((), (), s32[]{:S(2)}) async-start(), calls=%async_computation.4 | async-start | bytes 442368 | tf_op jit(solution)/shard_map/reduce_scatter | solution.py:120
  106.0 106.8 %all-gather.5.cloned.1.call-start = ((), (), s32[]{:S(2)}) async-start(), calls=%async_computation.5 | async-start | bytes 1622016 | tf_op jit(solution)/shard_map/all_gather | solution.py:124
  140.3 142.2 %reduce-scatter.5.cloned.1.call-start = ((), (), s32[]{:S(2)}) async-start(), calls=%async_computation.6 | async-start | bytes 3096576 | tf_op jit(solution)/shard_map/reduce_scatter | solution.py:134
  212.8 2.0 copy-start.1
  244.3 1.8 copy-start.4
Sparse Core Ops, SparseCore 0:
  26.5 76.6 all-gather.2
  106.1 32.6 reduce-scatter.2
  142.2 70.5 all-gather.4
  249.8 32.6 reduce-scatter.4
where the time goes:
time: 293 us; the launch traced here: 291 us
  waiting for transfers between devices  215 us (73%)
  blocking collectives  28.9 us (10%)
  matrix products  19.9 us (7%)
  between operations  14.6 us (5%)
  other arithmetic  10.4 us (4%)
    all_gather x1, waiting for transfers between devices, on_device(): lax.all_gather(head_rows, 'gy', axis=0, tiled=True)  76.7 us
    all_gather x1, waiting for transfers between devices, on_device(): lax.all_gather(stream, 'gy', axis=1, tiled=True).astype(jnp.float32)  72.5 us
    reduce_scatter x1, waiting for transfers between devices, on_device(): lax.psum_scatter(jnp.concatenate([gate, up], axis=1).astype(jnp.bfloat16)...  32.8 us
    reduce_scatter x1, waiting for transfers between devices, on_device(): lax.psum_scatter(partial_proj.astype(jnp.bfloat16), 'gx', scatter_dimensi...  32.8 us
    all_to_all x1, blocking collectives, on_device(): lax.all_to_all(normed, 'gx', split_axis=1, concat_axis=0, tiled=True)  28.9 us
    dot_general x4, matrix products, cache_part(): jnp.einsum('rtkgd,rkpd->rkgtp', queries, keys, preferred_element_type=jnp...  6.36 us
  transfers between devices with their start and end apart: 4, of which 4 were waited for; matrix products, arithmetic and copies ran while one was open for 0% of the time, Pallas kernels for 0%

commit v1 on v0

v1 whole, which is shorter than its diff:
```python
import jax
import jax.numpy as jnp
from jax import lax
from jax.experimental import pallas as pl
from jax.experimental.pallas import tpu as pltpu
from jax.sharding import PartitionSpec as P

MESH = pl.DeviceIdType.MESH
F32 = jnp.float32
BF16 = jnp.bfloat16

NX, NY, NZ, NC = 4, 4, 8, 2
ROLLS = 6
NEW = 4
GROUP = 8
HD = 128
CACHE = 2048
ROWS = 96
COLS = 256
FEAT = 1024
HID = 896
TILE = 128
CHUNKS = HID // TILE
D = 8192
SPLIT = 48
masked_score = -1e30
norm_eps = 1e-05
LAG = 2


def layer_kernel(
    len_ref,
    q_hbm,
    k_hbm,
    v_hbm,
    nk_hbm,
    nv_hbm,
    res_hbm,
    ow_hbm,
    gain_hbm,
    gw_hbm,
    uw_hbm,
    stream_hbm,
    act_hbm,
    q_v,
    k_v,
    v_v,
    nk_v,
    nv_v,
    res_v,
    ow_v,
    gain_v,
    w_v,
    ho,
    g1,
    g2,
    p1,
    r1,
    st_v,
    h_v,
    sx,
    sz,
    x_other,
    x_own,
    cp_s,
    cp_r,
    own,
    y_s,
    y_r,
    act_v,
    kv_sem,
    in_sem,
    w_sem,
    ag_send,
    ag_recv,
    r1_send,
    r1_recv,
    perm_sem,
    sx_sem,
    sz_sem,
    cp_sem,
    ys_sem,
    yr_sem,
    out_sem,
):
    gx = lax.axis_index("gx")
    gy = lax.axis_index("gy")
    y, c = lax.div(gx, NC), lax.rem(gx, NC)
    x, z = lax.div(gy, NZ), lax.rem(gy, NZ)

    def at_x(d):
        return (gx, lax.rem(x + d, NX) * NZ + z)

    def at_z(d):
        return (gx, x * NZ + lax.rem(z + d + NZ, NZ))

    def at_y(d):
        return (lax.rem(y + d, NY) * NC + c, gy)

    def slot(dx, dz):
        return lax.rem(x + dx, NX) * NZ + lax.rem(z + dz + NZ, NZ)

    partner = (y * NC + 1 - c, gy)
    perm = (lax.div(gy, 4), 4 * gx + lax.rem(gy, 4))
    moves = jnp.logical_or(perm[0] != gx, perm[1] != gy)

    barrier = pltpu.get_barrier_semaphore()

    def greet(device):
        pl.semaphore_signal(barrier, inc=1, device_id=device, device_id_type=MESH)

    for d in range(1, NX):
        greet(at_x(d))
    for d in range(1, NZ):
        greet(at_z(d))
    for d in range(1, NY * NC):
        greet((lax.rem(gx + d, NY * NC), gy))

    @pl.when(moves)
    def _():
        greet(perm)

    def local(src, dst, sem):
        return pltpu.make_async_copy(src, dst, sem)

    small = [
        local(q_hbm.at[pl.ds(gy * ROLLS, ROLLS)], q_v, in_sem.at[0]),
        local(nk_hbm, nk_v, in_sem.at[1]),
        local(nv_hbm, nv_v, in_sem.at[2]),
    ]
    for copy in small:
        copy.start()
    kcopy = [local(k_hbm.at[r, 0], k_v.at[r], kv_sem.at[0, r]) for r in range(ROLLS)]
    vcopy = [local(v_hbm.at[r, 0], v_v.at[r], kv_sem.at[1, r]) for r in range(ROLLS)]
    for r in range(ROLLS):
        kcopy[r].start()
        vcopy[r].start()
    later = [
        local(ow_hbm, ow_v, in_sem.at[3]),
        local(res_hbm, res_v, in_sem.at[4]),
        local(gain_hbm, gain_v, in_sem.at[5]),
    ]
    for copy in later:
        copy.start()
    wcopy = []
    for j in range(CHUNKS):
        cols = pl.ds(j * TILE, TILE)
        wcopy.append(local(gw_hbm.at[:, cols], w_v.at[j, :, pl.ds(0, TILE)], w_sem.at[0, j]))
        wcopy.append(local(uw_hbm.at[:, cols], w_v.at[j, :, pl.ds(TILE, TILE)], w_sem.at[1, j]))
    for copy in wcopy:
        copy.start()

    for copy in small:
        copy.wait()
    place = lax.broadcasted_iota(jnp.int32, (NEW * GROUP, CACHE), 1)
    row_id = lax.broadcasted_iota(jnp.int32, (NEW * GROUP, 1), 0)
    scale = HD ** (-0.5)
    for r in range(ROLLS):
        kcopy[r].wait()
        q32 = q_v[r].astype(F32).reshape(NEW * GROUP, HD)
        nk32 = nk_v[r].astype(F32)
        nv32 = nv_v[r].astype(F32)
        scores = (
            lax.dot_general(
                q32.astype(BF16), k_v[r], (((1,), (1,)), ((), ())), preferred_element_type=F32
            )
            * scale
        )
        length = len_ref[gy * ROLLS + r]
        scores = jnp.where(place < length, scores, masked_score)
        fresh = []
        for s in range(NEW):
            one = jnp.sum(q32 * nk32[s : s + 1, :], axis=1, keepdims=True) * scale
            fresh.append(jnp.where(row_id >= s * GROUP, one, masked_score))
        top = jnp.max(scores, axis=1, keepdims=True)
        for s in range(NEW):
            top = jnp.maximum(top, fresh[s])
        weights = jnp.exp(scores - top)
        total = jnp.sum(weights, axis=1, keepdims=True)
        vcopy[r].wait()
        mixed = jnp.dot(weights.astype(BF16), v_v[r], preferred_element_type=F32)
        for s in range(NEW):
            weight = jnp.exp(fresh[s] - top)
            total = total + weight
            mixed = mixed + weight.astype(BF16).astype(F32) * nv32[s : s + 1, :]
        ho[pl.ds(r * NEW * GROUP, NEW * GROUP), :] = mixed / total

    slabs = []
    for q in range(4):
        parts = [ho[pl.ds(2 * q + h, ROLLS * NEW, stride=GROUP), :] for h in range(2)]
        slabs.append(jnp.concatenate(parts, axis=1))
    g1[gy] = jnp.concatenate(slabs, axis=0).astype(BF16)

    peers = NX - 1 + NZ - 1 + NY * NC - 1

    @pl.when(moves)
    def _():
        pl.semaphore_wait(barrier, peers + 1)

    @pl.when(jnp.logical_not(moves))
    def _():
        pl.semaphore_wait(barrier, peers)

    part_rows = (pl.ds(0, SPLIT), pl.ds(SPLIT, ROWS - SPLIT))

    def gather(ref, phase):
        sent = []

        def send(part, origin, device):
            block = ref.at[origin, part_rows[part]]
            copy = pltpu.make_async_remote_copy(
                src_ref=block,
                dst_ref=block,
                send_sem=ag_send.at[phase, len(sent)],
                recv_sem=ag_recv.at[phase, part, origin],
                device_id=device,
                device_id_type=MESH,
            )
            copy.start()
            sent.append(copy)

        def arrive(part, origin):
            block = ref.at[origin, part_rows[part]]
            local(block, block, ag_recv.at[phase, part, origin]).wait()

        mine = slot(0, 0)
        send(0, mine, at_z(1))
        send(0, mine, at_z(-1))
        for d in (1, 3, 2):
            send(1, mine, at_x(d))
        send(1, mine, at_z(1))
        send(1, mine, at_z(-1))
        for d in (1, 3, 2):
            send(0, mine, at_x(d))
        for s in range(1, 5):
            up, down = slot(0, -s), slot(0, s)
            arrive(0, up)
            if s < 4:
                send(0, up, at_z(1))
            for d in (1, 3, 2):
                send(0, up, at_x(d))
            if s < 4:
                arrive(0, down)
                if s < 3:
                    send(0, down, at_z(-1))
                for d in (1, 3, 2):
                    send(0, down, at_x(d))
            for d in (0, 1, 3, 2):
                if s == 1 and d > 0:
                    here = slot(d, 0)
                    arrive(1, here)
                    send(1, here, at_z(1))
                    send(1, here, at_z(-1))
            for d in (0, 1, 3, 2):
                if s < 4:
                    up = slot(d, -s)
                    arrive(1, up)
                    if s < 3:
                        send(1, up, at_z(1))
                down = slot(d, s)
                arrive(1, down)
                if s < 4:
                    send(1, down, at_z(-1))
        for s in range(NZ):
            for d in (1, 3, 2):
                arrive(0, slot(d, s))
        return sent

    sent = gather(g1, 0)

    for copy in later:
        copy.wait()

    def project(i):
        got = g1[pl.ds(4 * i, 4)].astype(F32)
        slabs = [got[:, 24 * q : 24 * q + 24, :].reshape(ROWS, COLS) for q in range(4)]
        block = jnp.concatenate(slabs, axis=1).astype(BF16)
        return jnp.dot(block, ow_v[...], preferred_element_type=F32).astype(BF16)

    def r1_copy(step):
        i = lax.rem(gx + 1 + step, NY * NC)
        return pltpu.make_async_remote_copy(
            src_ref=p1.at[step],
            dst_ref=r1.at[6 - step],
            send_sem=r1_send.at[step],
            recv_sem=r1_recv.at[6 - step],
            device_id=(i, gy),
            device_id_type=MESH,
        )

    def project_step(step, carry):
        p1[step] = project(lax.rem(gx + 1 + step, NY * NC))
        r1_copy(step).start()
        return carry

    lax.fori_loop(0, NY * NC - 1, project_step, 0)
    summed = res_v[...].astype(F32) + project(gx).astype(F32)
    for t in range(NY * NC - 1):
        local(r1.at[t], r1.at[t], r1_recv.at[t]).wait()
        summed = summed + r1[t].astype(F32)
    stream = summed.astype(BF16)
    st_v[...] = stream
    stream_out = local(st_v, stream_hbm, out_sem.at[0])
    stream_out.start()
    stream32 = stream.astype(F32)
    gain = jnp.concatenate(
        [gain_v[pl.ds(2 * gy, 1), :], gain_v[pl.ds(2 * gy + 1, 1), :]], axis=1
    )
    h_v[...] = (stream32 * gain).astype(BF16)

    perm_copy = pltpu.make_async_remote_copy(
        src_ref=h_v,
        dst_ref=g2.at[perm[1]],
        send_sem=perm_sem.at[0],
        recv_sem=perm_sem.at[1],
        device_id=perm,
        device_id_type=MESH,
    )

    @pl.when(moves)
    def _():
        perm_copy.start()

    @pl.when(jnp.logical_not(moves))
    def _():
        g2[gy] = h_v[...]

    squares = jnp.sum(stream32 * stream32, axis=1, keepdims=True)
    squares = jnp.concatenate([squares, jnp.zeros((TILE - ROWS, 1), F32)], axis=0)
    wide = jnp.broadcast_to(squares, (TILE, TILE))
    sx[0] = jnp.transpose(wide)[0:8, :]

    def sx_copy(d):
        return pltpu.make_async_remote_copy(
            src_ref=sx.at[0],
            dst_ref=sx.at[d],
            send_sem=sx_sem.at[0, d],
            recv_sem=sx_sem.at[1, d],
            device_id=at_x(d),
            device_id_type=MESH,
        )

    def sz_copy(d):
        return pltpu.make_async_remote_copy(
            src_ref=sz.at[0],
            dst_ref=sz.at[d],
            send_sem=sz_sem.at[0, d],
            recv_sem=sz_sem.at[1, d],
            device_id=at_z(d),
            device_id_type=MESH,
        )

    for d in range(1, NX):
        sx_copy(d).start()

    @pl.when(moves)
    def _():
        perm_copy.wait_recv()

    sent = sent + gather(g2, 1)

    for d in range(1, NX):
        sx_copy(d).wait_recv()
    sz[0] = sx[0] + sx[1] + sx[2] + sx[3]
    for d in range(1, NZ):
        sz_copy(d).start()

    for d in range(NY):
        base = 2 * lax.rem(y + d, NY)
        for m in range(4):
            cols = pl.ds(COLS * m, COLS)
            x_other[pl.ds(ROWS * d, ROWS), cols] = g2[4 * (base + 1 - c) + m]
            x_own[pl.ds(ROWS * d, ROWS), cols] = g2[4 * (base + c) + m]
    for copy in wcopy:
        copy.wait()

    def cp_copy(j):
        return pltpu.make_async_remote_copy(
            src_ref=cp_s.at[j],
            dst_ref=cp_r.at[j],
            send_sem=cp_sem.at[0, j],
            recv_sem=cp_sem.at[1, j],
            device_id=partner,
            device_id_type=MESH,
        )

    def y_copy(d, j):
        return pltpu.make_async_remote_copy(
            src_ref=y_s.at[d - 1, j],
            dst_ref=y_r.at[d - 1, j],
            send_sem=ys_sem.at[d - 1, j],
            recv_sem=yr_sem.at[d - 1, j],
            device_id=at_y(d),
            device_id_type=MESH,
        )

    def multiply(j, carry):
        cp_s[j] = jnp.dot(x_other[...], w_v[j], preferred_element_type=F32).astype(BF16)
        cp_copy(j).start()
        own[j] = jnp.dot(x_own[...], w_v[j], preferred_element_type=F32)
        return carry

    def forward(j):
        cp_copy(j).wait_recv()
        for d in (1, 3, 2, 0):
            rows = pl.ds(ROWS * d, ROWS)
            both = own[j, rows, :] + cp_r[j, rows, :].astype(F32)
            if d == 0:
                own[j, rows, :] = both
            else:
                y_s[d - 1, j] = both.astype(BF16)
                y_copy(d, j).start()

    def multiply_forward(j, carry):
        multiply(j, carry)
        forward(j - LAG)
        return carry

    def forward_only(j, carry):
        forward(j)
        return carry

    lax.fori_loop(0, LAG, multiply, 0)
    lax.fori_loop(LAG, CHUNKS, multiply_forward, 0)
    lax.fori_loop(CHUNKS - LAG, CHUNKS, forward_only, 0)

    total = sz[0]
    for d in range(1, NZ):
        sz_copy(d).wait_recv()
        total = total + sz[d]
    tall = jnp.transpose(jnp.broadcast_to(total[0:1, :], (TILE, TILE)))[0:ROWS, :]
    factor = lax.rsqrt(tall / D + norm_eps)

    def finish(j, carry):
        both = own[j, pl.ds(0, ROWS), :]
        for d in (1, 3, 2):
            y_copy(d, j).wait_recv()
            both = both + y_r[d - 1, j].astype(F32)
        gate = both[:, :TILE] * factor
        up = both[:, TILE:] * factor
        cols = pl.ds(pl.multiple_of(j * TILE, TILE), TILE)
        act_v[:, cols] = (gate / (1.0 + jnp.exp(-gate)) * up).astype(BF16)
        return carry

    lax.fori_loop(0, CHUNKS, finish, 0)
    act_out = local(act_v, act_hbm, out_sem.at[1])
    act_out.start()

    for copy in sent:
        copy.wait_send()

    def close_r1(step, carry):
        r1_copy(step).wait_send()
        return carry

    lax.fori_loop(0, NY * NC - 1, close_r1, 0)

    @pl.when(moves)
    def _():
        perm_copy.wait_send()

    for d in range(1, NX):
        sx_copy(d).wait_send()
    for d in range(1, NZ):
        sz_copy(d).wait_send()

    def close_chunk(j, carry):
        cp_copy(j).wait_send()
        for d in (1, 2, 3):
            y_copy(d, j).wait_send()
        return carry

    lax.fori_loop(0, CHUNKS, close_chunk, 0)
    stream_out.wait()
    act_out.wait()


def on_device(
    query,
    cache_key,
    cache_value,
    new_key,
    new_value,
    prefix_len,
    residual,
    out_weight,
    norm_gain,
    gate_weight,
    up_weight,
):
    anywhere = pl.BlockSpec(memory_space=pl.ANY)
    vmem = pltpu.VMEM
    dma = pltpu.SemaphoreType.DMA
    return pl.pallas_call(
        layer_kernel,
        name="decoder_layer",
        out_shape=(
            jax.ShapeDtypeStruct((ROWS, COLS), BF16),
            jax.ShapeDtypeStruct((ROWS, HID), BF16),
        ),
        in_specs=[pl.BlockSpec(memory_space=pltpu.SMEM)] + [anywhere] * 10,
        out_specs=(anywhere, anywhere),
        scratch_shapes=[
            vmem((ROLLS, NEW, GROUP, HD), BF16),
            vmem((ROLLS, CACHE, HD), BF16),
            vmem((ROLLS, CACHE, HD), BF16),
            vmem((ROLLS, NEW, HD), BF16),
            vmem((ROLLS, NEW, HD), BF16),
            vmem((ROWS, COLS), BF16),
            vmem((FEAT, COLS), BF16),
            vmem((D // TILE, TILE), F32),
            vmem((CHUNKS, FEAT, 2 * TILE), BF16),
            vmem((ROLLS * NEW * GROUP, HD), F32),
            vmem((NX * NZ, ROWS, COLS), BF16),
            vmem((NX * NZ, ROWS, COLS), BF16),
            vmem((7, ROWS, COLS), BF16),
            vmem((7, ROWS, COLS), BF16),
            vmem((ROWS, COLS), BF16),
            vmem((ROWS, COLS), BF16),
            vmem((NX, 8, TILE), F32),
            vmem((NZ, 8, TILE), F32),
            vmem((4 * ROWS, FEAT), BF16),
            vmem((4 * ROWS, FEAT), BF16),
            vmem((CHUNKS, 4 * ROWS, 2 * TILE), BF16),
            vmem((CHUNKS, 4 * ROWS, 2 * TILE), BF16),
            vmem((CHUNKS, 4 * ROWS, 2 * TILE), F32),
            vmem((3, CHUNKS, ROWS, 2 * TILE), BF16),
            vmem((3, CHUNKS, ROWS, 2 * TILE), BF16),
            vmem((ROWS, HID), BF16),
            dma((2, ROLLS)),
            dma((6,)),
            dma((2, CHUNKS)),
            dma((2, 62)),
            dma((2, 2, 32)),
            dma((7,)),
            dma((7,)),
            dma((2,)),
            dma((2, NX)),
            dma((2, NZ)),
            dma((2, CHUNKS)),
            dma((3, CHUNKS)),
            dma((3, CHUNKS)),
            dma((2,)),
        ],
        compiler_params=pltpu.CompilerParams(
            collective_id=0, has_side_effects=True, vmem_limit_bytes=50 * 2**20
        ),
    )(
        prefix_len,
        query,
        cache_key,
        cache_value,
        new_key.reshape(ROLLS, NEW, HD),
        new_value.reshape(ROLLS, NEW, HD),
        residual,
        out_weight,
        norm_gain.reshape(D // TILE, TILE),
        gate_weight,
        up_weight,
    )


def solution(mesh):
    in_specs = (
        P(None, None, "gx", None),
        P("gy", "gx", None, None),
        P("gy", "gx", None, None),
        P("gy", None, "gx", None),
        P("gy", None, "gx", None),
        P(),
        P("gx", "gy"),
        P("gx", "gy"),
        P(),
        P("gx", "gy"),
        P("gx", "gy"),
    )
    out_specs = (P("gx", "gy"), P("gx", "gy"))
    return jax.shard_map(
        on_device, mesh=mesh, in_specs=in_specs, out_specs=out_specs, check_vma=False
    )
```

time: 293 us -> 93.7 us (0.32)
  waiting for transfers between devices: 215 us -> 0 us
  Pallas kernels: 0 us -> 84.6 us
  blocking collectives: 28.9 us -> 0 us
  matrix products: 19.9 us -> 0 us
  between operations: 14.6 us -> 0.66 us
  other arithmetic: 10.4 us -> 0 us
  local copies, waits for them, and re-layouts: 1.66 us -> 7.35 us
    all_gather x2 -> x0, waiting for transfers between devices: 149 us -> none  [the longest x1 76.7 us: on_device(): lax.all_gather(head_rows, 'gy', axis=0, tiled=True)]
    pallas_call x0 -> x1, Pallas kernels: none -> 84.6 us  [on_device(): pl.pallas_call(layer_kernel, name='decoder_layer', out_shape=(jax.ShapeDt...]
    reduce_scatter x2 -> x0, waiting for transfers between devices: 65.6 us -> none  [the longest x1 32.8 us: on_device(): lax.psum_scatter(jnp.concatenate([gate, up], axis=1).astype(jnp.bfloat16)...]
    all_to_all x1 -> x0, blocking collectives: 28.9 us -> none  [on_device(): lax.all_to_all(normed, 'gx', split_axis=1, concat_axis=0, tiled=True)]
    dot_general x13 -> x0, matrix products: 19.9 us -> none  [the longest x4 6.36 us: cache_part(): jnp.einsum('rtkgd,rkpd->rkgtp', queries, keys, preferred_element_type=jnp...]
    unnamed x17 -> x16, local copies, waits for them, and re-layouts: 0.68 us -> 7.35 us
    convert_element_type x4 -> x0, other arithmetic: 3.68 us -> none  [the longest x1 1.43 us: on_device(): stream = (residual.astype(jnp.float32) + summed).astype(jnp.bfloat16)]
    reduce_sum x6 -> x0, other arithmetic: 2.97 us -> none  [the longest x1 1.93 us: on_device(): jnp.mean(full_rows * full_rows, axis=-1, keepdims=True) + norm_eps]
  transfers between devices with their start and end apart: 4 -> 0, of which waited for: 4 -> 0; matrix products, arithmetic and copies ran while one was open for 0% -> 0% of each run, Pallas kernels for 0% -> 0%
where the time goes in v1:
time: 93.7 us; the launch traced here: 92.6 us
  Pallas kernels  84.6 us (90%)
  local copies, waits for them, and re-layouts  7.35 us (8%)
    pallas_call x1, Pallas kernels, on_device(): pl.pallas_call(layer_kernel, name='decoder_layer', out_shape=(jax.ShapeDt...  84.6 us
    unnamed x16, local copies, waits for them, and re-layouts  7.35 us

profile of v1, /device:TPU:1, one launch (start us, length us, event | category | flops | bytes accessed | tf_op | source)
XLA Modules:
  0.0 92.6 jit_solution(5504552630820399901)
XLA Ops:
  0.6 0.0 copy-start
  0.6 1.4 %copy-done = bf16[192,4,8,128]{3,2,1,0:T(8,128)(2,1)S(1)} copy-done((bf16[192,4,8,128]{3,2,1,0:T(8,128)(2,1)S(1)}, bf16[192,4,8,128]{3,2,1,0:T(8,128)(2,1)}, u32[]{:S(2)}) %copy-start) | copy-done | bytes 1572888
  2.0 0.0 copy-start.1
  2.0 1.0 %copy-done.1 = bf16[1024,256]{1,0:T(8,128)(2,1)S(1)} copy-done((bf16[1024,256]{1,0:T(8,128)(2,1)S(1)}, bf16[1024,256]{1,0:T(8,128)(2,1)}, u32[]{:S(2)}) %copy-start.1) | copy-done | bytes 524312
  3.1 0.0 copy-start.2
  3.1 0.8 copy-done.2
  3.9 0.0 copy-start.3
  3.9 0.8 copy-done.3
  4.6 0.0 copy-start.4
  4.6 0.7 copy-done.4
  5.3 0.0 copy-start.5
  5.3 0.7 copy-done.5
  6.0 0.0 copy-start.6
  6.0 0.7 copy-done.6
  6.7 84.6 %decoder_layer.1 = (bf16[96,256]{1,0:T(8,128)(2,1)S(1)}, bf16[96,896]{1,0:T(8,128)(2,1)S(1)}) custom-call(s32[192]{0:T(256)S(1)} %copy-done.6, bf16[192,4,8,128]{3,2,1,0:T(8,128)(2,1)S(1)} %copy-done, bf16[6,1,2048,128]{3,2,1,0:T(8,128)(2,1)} %k_hbm.1, bf16[6,1,2048,128]{3,2,1,0:T(8,128)(2,1)} %v_hbm.1, bf16[6,4,128]{2,1,0:T(4,128)(2,1)S(1)} %bitcast.4, ...), custom_call_target="tpu_custom_call" | custom-call | tf_op jit(solution)/shard_map/decoder_layer/pallas_call | solution.py:494
  91.3 0.6 copy.15
  91.9 0.7 copy.16
Async XLA Ops:
  0.6 1.4 %copy-start = (bf16[192,4,8,128]{3,2,1,0:T(8,128)(2,1)S(1)}, bf16[192,4,8,128]{3,2,1,0:T(8,128)(2,1)}, u32[]{:S(2)}) copy-start(bf16[192,4,8,128]{3,2,1,0:T(8,128)(2,1)} %q_hbm.1) | copy-start | bytes 4718596
  2.0 1.0 %copy-start.1 = (bf16[1024,256]{1,0:T(8,128)(2,1)S(1)}, bf16[1024,256]{1,0:T(8,128)(2,1)}, u32[]{:S(2)}) copy-start(bf16[1024,256]{1,0:T(8,128)(2,1)} %ow_hbm.1) | copy-start | bytes 1572868
  3.1 0.8 copy-start.2
  3.9 0.8 copy-start.3
  4.6 0.7 copy-start.4
  5.3 0.7 copy-start.5
  6.0 0.7 copy-start.6

commit v2 on v1

v2 whole, which is shorter than its diff:
```python
import jax
import jax.numpy as jnp
from jax import lax
from jax.experimental import pallas as pl
from jax.experimental.pallas import tpu as pltpu
from jax.sharding import PartitionSpec as P

MESH = pl.DeviceIdType.MESH
F32 = jnp.float32
BF16 = jnp.bfloat16

NX, NY, NZ, NC = 4, 4, 8, 2
ROLLS = 6
NEW = 4
GROUP = 8
HD = 128
CACHE = 2048
ROWS = 96
COLS = 256
FEAT = 1024
HID = 896
TILE = 128
CHUNKS = HID // TILE
D = 8192
masked_score = -1e30
norm_eps = 1e-05
PER = (24,)
BLOCK = (96,)
FIRST = (0,)
BASE = (0,)
PARTS = len(PER)
SPLIT = ((80, 16),)
LAG = 2
LAG2 = 5
STEP = 2


def layer_kernel(
    len_hbm,
    q_hbm,
    k_hbm,
    v_hbm,
    nk_hbm,
    nv_hbm,
    res_hbm,
    ow_hbm,
    gain_hbm,
    gw_hbm,
    uw_hbm,
    stream_hbm,
    act_hbm,
    len_ref,
    q_v,
    k_v,
    v_v,
    nk_v,
    nv_v,
    res_v,
    ow_v,
    gain_v,
    w_v,
    ho,
    g1,
    g2,
    x_heads,
    p1,
    r1,
    st_v,
    h_v,
    sx,
    sz,
    x_other,
    x_own,
    cp_s,
    cp_r,
    own,
    y_s,
    y_r,
    act_f,
    act_v,
    kv_sem,
    in_sem,
    w_sem,
    ag_send,
    ag_recv,
    agx_recv,
    agz_recv,
    r1_send,
    r1_recv,
    perm_sem,
    sx_sem,
    sz_sem,
    cp_sem,
    ys_sem,
    yr_sem,
    out_sem,
):
    gx = lax.axis_index("gx")
    gy = lax.axis_index("gy")
    y, c = lax.div(gx, NC), lax.rem(gx, NC)
    x, z = lax.div(gy, NZ), lax.rem(gy, NZ)

    xs = [lax.rem(x + d, NX) for d in range(NX)]
    ys = [lax.rem(y + d, NY) for d in range(NY)]
    zs = [lax.rem(z + d, NZ) for d in range(NZ)]
    x_line = [(gx, xx * NZ + z) for xx in xs]
    z_line = [(gx, x * NZ + zz) for zz in zs]

    def at_x(d):
        return x_line[d]

    def at_z(d):
        return z_line[d]

    def at_y(d):
        yy = ys[d] if isinstance(d, int) else lax.rem(y + d, NY)
        return (yy * NC + c, gy)

    partner = (y * NC + 1 - c, gy)
    perm = (lax.div(gy, 4), 4 * gx + lax.rem(gy, 4))
    moves = jnp.logical_or(perm[0] != gx, perm[1] != gy)

    barrier = pltpu.get_barrier_semaphore()

    def greet(device):
        pl.semaphore_signal(barrier, inc=1, device_id=device, device_id_type=MESH)

    for d in range(1, NX):
        greet(at_x(d))
    for d in range(1, NZ):
        greet(at_z(d))
    for d in range(1, NY * NC):
        greet((lax.rem(gx + d, NY * NC), gy))

    @pl.when(moves)
    def _():
        greet(perm)

    def local(src, dst, sem):
        return pltpu.make_async_copy(src, dst, sem)

    small = [
        local(len_hbm, len_ref, in_sem.at[6]),
        local(q_hbm.at[pl.ds(gy * ROLLS, ROLLS)], q_v, in_sem.at[0]),
        local(nk_hbm, nk_v, in_sem.at[1]),
        local(nv_hbm, nv_v, in_sem.at[2]),
    ]
    for copy in small:
        copy.start()
    kcopy = [local(k_hbm.at[r, 0], k_v.at[r], kv_sem.at[0, r]) for r in range(ROLLS)]
    vcopy = [local(v_hbm.at[r, 0], v_v.at[r], kv_sem.at[1, r]) for r in range(ROLLS)]
    for r in range(ROLLS):
        kcopy[r].start()
        vcopy[r].start()
    later = [
        local(ow_hbm, ow_v, in_sem.at[3]),
        local(res_hbm, res_v, in_sem.at[4]),
        local(gain_hbm, gain_v, in_sem.at[5]),
    ]
    for copy in later:
        copy.start()
    wcopy = []
    for j in range(CHUNKS):
        cols = pl.ds(j * TILE, TILE)
        wcopy.append(local(gw_hbm.at[:, cols], w_v.at[j, :, pl.ds(0, TILE)], w_sem.at[0, j]))
        wcopy.append(local(uw_hbm.at[:, cols], w_v.at[j, :, pl.ds(TILE, TILE)], w_sem.at[1, j]))
    for copy in wcopy:
        copy.start()

    closers = []

    def close_all():
        for close in closers:
            close()

    for copy in small:
        copy.wait()
    place = lax.broadcasted_iota(jnp.int32, (NEW * GROUP, CACHE), 1)
    row_id = lax.broadcasted_iota(jnp.int32, (NEW * GROUP, 1), 0)
    scale = HD ** (-0.5)

    def attend(group):
        for r in group:
            kcopy[r].wait()
            vcopy[r].wait()
        for r in group:
            q32 = q_v[r].astype(F32).reshape(NEW * GROUP, HD)
            nk32 = nk_v[r].astype(F32)
            nv32 = nv_v[r].astype(F32)
            scores = (
                lax.dot_general(
                    q32.astype(BF16),
                    k_v[r],
                    (((1,), (1,)), ((), ())),
                    preferred_element_type=F32,
                )
                * scale
            )
            length = len_ref[gy * ROLLS + r]
            scores = jnp.where(place < length, scores, masked_score)
            fresh = []
            for s in range(NEW):
                one = jnp.sum(q32 * nk32[s : s + 1, :], axis=1, keepdims=True) * scale
                fresh.append(jnp.where(row_id >= s * GROUP, one, masked_score))
            top = jnp.max(scores, axis=1, keepdims=True)
            for s in range(NEW):
                top = jnp.maximum(top, fresh[s])
            weights = jnp.exp(scores - top)
            total = jnp.sum(weights, axis=1, keepdims=True)
            mixed = jnp.dot(weights.astype(BF16), v_v[r], preferred_element_type=F32)
            for s in range(NEW):
                weight = jnp.exp(fresh[s] - top)
                total = total + weight
                mixed = mixed + weight.astype(BF16).astype(F32) * nv32[s : s + 1, :]
            ho[pl.ds(r * NEW * GROUP, NEW * GROUP), :] = mixed / total

    for start in range(0, ROLLS, STEP):
        attend(range(start, start + STEP))

    slabs = []
    for q in range(PARTS):
        for slab in range(4):
            parts = [
                ho[pl.ds(8 * 16 * q + 2 * slab + h, PER[q], stride=GROUP), :] for h in range(2)
            ]
            slabs.append(jnp.concatenate(parts, axis=1))
    g1[x, z] = jnp.concatenate(slabs, axis=0).astype(BF16)

    peers = NX - 1 + NZ - 1 + NY * NC - 1

    @pl.when(moves)
    def _():
        pl.semaphore_wait(barrier, peers + 1)

    @pl.when(jnp.logical_not(moves))
    def _():
        pl.semaphore_wait(barrier, peers)

    def gather(ref, phase, first, rows_a, rows_b):
        part_a, part_b = pl.ds(first, rows_a), pl.ds(first + rows_a, rows_b)
        along_z = (1, 7, 2, 6, 3, 5, 4)
        along_x = (1, 3, 2)
        count = [0]

        def send(block, sem, device):
            copy = pltpu.make_async_remote_copy(
                src_ref=block,
                dst_ref=block,
                send_sem=ag_send.at[phase, count[0]],
                recv_sem=sem,
                device_id=device,
                device_id_type=MESH,
            )
            copy.start()
            count[0] += 1
            closers.append(copy.wait_send)

        def piece_a(dx, zz):
            xx = xs[dx]
            return ref.at[xx, zz, part_a], ag_recv.at[phase, xx, zz]

        def piece_b(dx):
            xx = xs[dx]
            return ref.at[xx, z, part_b], agx_recv.at[phase, xx]

        def piece_all(d):
            zz = zs[d]
            return ref.at[:, zz, part_b], agz_recv.at[phase, zz]

        def arrive(block, sem):
            local(block, block, sem).wait()

        for d in along_z:
            send(*piece_a(0, z), at_z(d))
        for d in along_x:
            if rows_b:
                send(*piece_b(0), at_x(d))
        for d in along_x:
            send(*piece_a(0, z), at_x(d))
        yield
        if rows_b:
            for d in along_x:
                arrive(*piece_b(d))
            for d in along_z:
                send(*piece_all(0), at_z(d))
        yield
        for d in along_z:
            piece = piece_a(0, zs[NZ - d])
            arrive(*piece)
            for e in along_x:
                send(*piece, at_x(e))
        yield
        if rows_b:
            for d in along_z:
                arrive(*piece_all(d))
        near = lax.div(z, 4)
        for zz in range(4):
            for d in along_x:
                arrive(*piece_a(d, 4 * near + zz))
        yield
        for zz in range(4):
            for d in along_x:
                arrive(*piece_a(d, 4 * (1 - near) + zz))
        yield

    heads = [gather(g1, q, FIRST[q], *SPLIT[q]) for q in range(PARTS)]
    for step in range(3):
        for q in range(PARTS):
            next(heads[q])

    for copy in later:
        copy.wait()

    def part_of(q):
        return pl.ds(FIRST[q], BLOCK[q])

    def r1_copy(q, n, half, d):
        place = 2 * d + lax.rem(half + c, 2)
        return pltpu.make_async_remote_copy(
            src_ref=p1.at[n, d, part_of(q)],
            dst_ref=r1.at[place, part_of(q)],
            send_sem=r1_send.at[q, n, d],
            recv_sem=r1_recv.at[q, place],
            device_id=(2 * ys[d] + half, gy),
            device_id_type=MESH,
        )

    def project(q, n, half):
        per, size = PER[q], BLOCK[q]
        for d in range(NY):
            got = g1[ys[d], pl.ds(4 * half, 4), part_of(q), :].astype(F32)
            slabs = [
                got[:, per * i : per * i + per, :].reshape(size, COLS) for i in range(4)
            ]
            x_heads[pl.ds(size * d, size), :] = jnp.concatenate(slabs, axis=1).astype(BF16)
        rows = x_heads[pl.ds(0, 4 * size), :]
        part = jnp.dot(rows, ow_v[...], preferred_element_type=F32).astype(BF16)
        for d in (2, 1, 3, 0):
            p1[n, d, part_of(q)] = part[size * d : size * d + size, :]
            if d > 0:
                r1_copy(q, n, half, d).start()
                closers.append(r1_copy(q, n, half, d).wait_send)
        crosses = lax.rem(half + c, 2) == 1

        @pl.when(crosses)
        def _():
            r1_copy(q, n, half, 0).start()

        @pl.when(jnp.logical_not(crosses))
        def _():
            r1[0, part_of(q)] = p1[n, 0, part_of(q)]

        def close():
            @pl.when(crosses)
            def _():
                r1_copy(q, n, half, 0).wait_send()

        closers.append(close)

    near = lax.div(z, 4)

    def project_all(q):
        next(heads[q])
        project(q, 0, near)
        next(heads[q])
        project(q, 1, 1 - near)

    def perm_copy(q):
        return pltpu.make_async_remote_copy(
            src_ref=h_v.at[part_of(q)],
            dst_ref=g2.at[lax.div(perm[1], NZ), lax.rem(perm[1], NZ), part_of(q)],
            send_sem=perm_sem.at[0, q],
            recv_sem=perm_sem.at[1, q],
            device_id=perm,
            device_id_type=MESH,
        )

    def reduce(q):
        residual = res_v[...].astype(F32)
        at, per = 16 * q, PER[q]
        summed = jnp.concatenate(
            [residual[24 * b + at : 24 * b + at + per, :] for b in range(4)], axis=0
        )
        for t in range(NY * NC):
            if t > 0:
                piece = r1.at[t, part_of(q)]
                local(piece, piece, r1_recv.at[q, t]).wait()
            summed = summed + r1[t, part_of(q), :].astype(F32)
        stream32 = summed.astype(BF16).astype(F32)
        h_v[part_of(q), :] = (stream32 * gain).astype(BF16)

        @pl.when(moves)
        def _():
            perm_copy(q).start()

        @pl.when(jnp.logical_not(moves))
        def _():
            g2[x, z, part_of(q)] = h_v[part_of(q), :]

        def close():
            @pl.when(moves)
            def _():
                perm_copy(q).wait_send()

        closers.append(close)
        return stream32

    def arrived(q):
        @pl.when(moves)
        def _():
            perm_copy(q).wait_recv()

    def sx_copy(d):
        return pltpu.make_async_remote_copy(
            src_ref=sx.at[0],
            dst_ref=sx.at[d],
            send_sem=sx_sem.at[0, d],
            recv_sem=sx_sem.at[1, d],
            device_id=at_x(d),
            device_id_type=MESH,
        )

    def sz_copy(d):
        return pltpu.make_async_remote_copy(
            src_ref=sz.at[0],
            dst_ref=sz.at[d],
            send_sem=sz_sem.at[0, d],
            recv_sem=sz_sem.at[1, d],
            device_id=at_z(d),
            device_id_type=MESH,
        )

    gain = jnp.concatenate(
        [gain_v[pl.ds(2 * gy, 1), :], gain_v[pl.ds(2 * gy + 1, 1), :]], axis=1
    )
    rows32 = []
    for q in range(PARTS):
        project_all(q)
    for q in range(PARTS):
        rows32.append(reduce(q))
    halves = [gather(g2, PARTS + q, FIRST[q], *SPLIT[q]) for q in range(PARTS)]
    for q in range(PARTS):
        arrived(q)
        next(halves[q])

    squares = [jnp.sum(rows * rows, axis=1, keepdims=True) for rows in rows32]
    squares = jnp.concatenate(squares + [jnp.zeros((TILE - ROWS, 1), F32)], axis=0)
    sx[0] = jnp.transpose(jnp.broadcast_to(squares, (TILE, TILE)))[0:8, :]
    for d in range(1, NX):
        sx_copy(d).start()
        closers.append(sx_copy(d).wait_send)
    pieces = []
    for b in range(4):
        for q in range(PARTS):
            pieces.append(rows32[q][PER[q] * b : PER[q] * (b + 1), :])
    st_v[...] = jnp.concatenate(pieces, axis=0).astype(BF16)
    stream_out = local(st_v, stream_hbm, out_sem.at[0])
    stream_out.start()
    for step in range(2):
        for q in range(PARTS):
            next(halves[q])
    for d in range(1, NX):
        sx_copy(d).wait_recv()
    sz[0] = sx[0] + sx[1] + sx[2] + sx[3]
    for d in range(1, NZ):
        sz_copy(d).start()
        closers.append(sz_copy(d).wait_send)

    for copy in wcopy:
        copy.wait()

    def core_rows(h):
        return pl.ds(BASE[h], 4 * BLOCK[h])

    def cp_copy(h, j):
        return pltpu.make_async_remote_copy(
            src_ref=cp_s.at[j, core_rows(h)],
            dst_ref=cp_r.at[j, core_rows(h)],
            send_sem=cp_sem.at[0, h, j],
            recv_sem=cp_sem.at[1, h, j],
            device_id=partner,
            device_id_type=MESH,
        )

    def via(h, j):
        return 1 + 2 * lax.rem(j + h, 2)

    def y_copy(h, d, j, to):
        return pltpu.make_async_remote_copy(
            src_ref=y_s.at[d - 1, j, part_of(h)],
            dst_ref=y_r.at[d - 1, j, part_of(h)],
            send_sem=ys_sem.at[h, d - 1, j],
            recv_sem=yr_sem.at[h, d - 1, j],
            device_id=at_y(to),
            device_id_type=MESH,
        )

    def y_rows(h, d):
        return pl.ds(pl.multiple_of(BASE[h] + BLOCK[h] * d, 16), BLOCK[h])

    def run(h):
        size = BLOCK[h]
        for d in range(NY):
            yy = ys[d]
            rows = pl.ds(BASE[h] + size * d, size)
            for m in range(4):
                cols = pl.ds(COLS * m, COLS)
                x_other[rows, cols] = g2[yy, 4 * (1 - c) + m, part_of(h)]
                x_own[rows, cols] = g2[yy, 4 * c + m, part_of(h)]

        def multiply(j):
            other = jnp.dot(x_other[core_rows(h), :], w_v[j], preferred_element_type=F32)
            cp_s[j, core_rows(h)] = other.astype(BF16)
            cp_copy(h, j).start()
            own[j, core_rows(h)] = jnp.dot(
                x_own[core_rows(h), :], w_v[j], preferred_element_type=F32
            )

        def add_cores(j):
            cp_copy(h, j).wait_recv()
            both = own[j, core_rows(h), :] + cp_r[j, core_rows(h), :].astype(F32)
            own[j, core_rows(h)] = both
            y_s[1, j, part_of(h)] = both[2 * size : 3 * size, :].astype(BF16)
            y_copy(h, 2, j, via(h, j)).start()
            direct = 4 - via(h, j)
            y_s[direct - 1, j, part_of(h)] = own[j, y_rows(h, direct), :].astype(BF16)
            y_copy(h, direct, j, direct).start()

        def add_relay(j):
            y_copy(h, 2, j, via(h, j)).wait_recv()
            d = via(h, j)
            both = own[j, y_rows(h, d), :] + y_r[1, j, part_of(h), :].astype(F32)
            y_s[d - 1, j, part_of(h)] = both.astype(BF16)
            y_copy(h, d, j, d).start()

        def step(j, carry):
            @pl.when(j < CHUNKS)
            def _():
                multiply(j)

            @pl.when(jnp.logical_and(j >= LAG, j < CHUNKS + LAG))
            def _():
                add_cores(j - LAG)

            @pl.when(j >= LAG2)
            def _():
                add_relay(j - LAG2)

            return carry

        lax.fori_loop(0, CHUNKS + LAG2, step, 0)

        def close_chunks():
            def close(j, carry):
                cp_copy(h, j).wait_send()
                y_copy(h, 1, j, 1).wait_send()
                y_copy(h, 2, j, via(h, j)).wait_send()
                y_copy(h, 3, j, 3).wait_send()
                return carry

            lax.fori_loop(0, CHUNKS, close, 0)

        closers.append(close_chunks)

    for q in range(PARTS):
        next(halves[q])
        next(halves[q])
        run(q)

    total = sz[0]
    for d in range(1, NZ):
        sz_copy(d).wait_recv()
        total = total + sz[d]
    tall = jnp.transpose(jnp.broadcast_to(total[0:1, :], (TILE, TILE)))[0:ROWS, :]
    factor = lax.rsqrt(tall / D + norm_eps)

    def finish(h):
        size, per = BLOCK[h], PER[h]

        def tile(j, carry):
            both = own[j, pl.ds(BASE[h], size), :]
            for d in (1, 3):
                y_copy(h, d, j, d).wait_recv()
                both = both + y_r[d - 1, j, part_of(h), :].astype(F32)
            here = factor[FIRST[h] : FIRST[h] + size, :]
            gate = both[:, :TILE] * here
            up = both[:, TILE:] * here
            result = gate / (1.0 + jnp.exp(-gate)) * up
            cols = pl.ds(pl.multiple_of(j * TILE, TILE), TILE)
            for b in range(4):
                act_f[pl.ds(24 * b + 16 * h, per), cols] = result[per * b : per * b + per, :]
            return carry

        lax.fori_loop(0, CHUNKS, tile, 0)

    for q in range(PARTS):
        finish(q)
    act_v[...] = act_f[...].astype(BF16)
    act_out = local(act_v, act_hbm, out_sem.at[1])
    act_out.start()
    closers.append(act_out.wait)
    closers.append(stream_out.wait)
    close_all()


def on_device(
    query,
    cache_key,
    cache_value,
    new_key,
    new_value,
    prefix_len,
    residual,
    out_weight,
    norm_gain,
    gate_weight,
    up_weight,
):
    anywhere = pl.BlockSpec(memory_space=pltpu.HBM)
    vmem = pltpu.VMEM
    dma = pltpu.SemaphoreType.DMA
    return pl.pallas_call(
        layer_kernel,
        name="decoder_layer",
        out_shape=(
            jax.ShapeDtypeStruct((ROWS, COLS), BF16),
            jax.ShapeDtypeStruct((ROWS, HID), BF16),
        ),
        in_specs=[anywhere] * 11,
        out_specs=(anywhere, anywhere),
        scratch_shapes=[
            pltpu.SMEM((ROLLS * NX * NZ,), jnp.int32),
            vmem((ROLLS, NEW, GROUP, HD), BF16),
            vmem((ROLLS, CACHE, HD), BF16),
            vmem((ROLLS, CACHE, HD), BF16),
            vmem((ROLLS, NEW, HD), BF16),
            vmem((ROLLS, NEW, HD), BF16),
            vmem((ROWS, COLS), BF16),
            vmem((FEAT, COLS), BF16),
            vmem((D // TILE, TILE), F32),
            vmem((CHUNKS, FEAT, 2 * TILE), BF16),
            vmem((ROLLS * NEW * GROUP, HD), F32),
            vmem((NX, NZ, ROWS, COLS), BF16),
            vmem((NX, NZ, ROWS, COLS), BF16),
            vmem((4 * ROWS, FEAT), BF16),
            vmem((2, NY, ROWS, COLS), BF16),
            vmem((NY * NC, ROWS, COLS), BF16),
            vmem((ROWS, COLS), BF16),
            vmem((ROWS, COLS), BF16),
            vmem((NX, 8, TILE), F32),
            vmem((NZ, 8, TILE), F32),
            vmem((4 * ROWS, FEAT), BF16),
            vmem((4 * ROWS, FEAT), BF16),
            vmem((CHUNKS, 4 * ROWS, 2 * TILE), BF16),
            vmem((CHUNKS, 4 * ROWS, 2 * TILE), BF16),
            vmem((CHUNKS, 4 * ROWS, 2 * TILE), F32),
            vmem((3, CHUNKS, ROWS, 2 * TILE), BF16),
            vmem((3, CHUNKS, ROWS, 2 * TILE), BF16),
            vmem((ROWS, HID), F32),
            vmem((ROWS, HID), BF16),
            dma((2, ROLLS)),
            dma((7,)),
            dma((2, CHUNKS)),
            dma((2 * PARTS, 41)),
            dma((2 * PARTS, NX, NZ)),
            dma((2 * PARTS, NX)),
            dma((2 * PARTS, NZ)),
            dma((2, 2, NY)),
            dma((2, NY * NC)),
            dma((2, 2)),
            dma((2, NX)),
            dma((2, NZ)),
            dma((2, 2, CHUNKS)),
            dma((2, 3, CHUNKS)),
            dma((2, 3, CHUNKS)),
            dma((3,)),
        ],
        compiler_params=pltpu.CompilerParams(
            collective_id=0, has_side_effects=True, vmem_limit_bytes=63 * 2**20
        ),
    )(
        prefix_len,
        query,
        cache_key,
        cache_value,
        new_key.reshape(ROLLS, NEW, HD),
        new_value.reshape(ROLLS, NEW, HD),
        residual,
        out_weight,
        norm_gain.reshape(D // TILE, TILE),
        gate_weight,
        up_weight,
    )


def solution(mesh):
    in_specs = (
        P(None, None, "gx", None),
        P("gy", "gx", None, None),
        P("gy", "gx", None, None),
        P("gy", None, "gx", None),
        P("gy", None, "gx", None),
        P(),
        P("gx", "gy"),
        P("gx", "gy"),
        P(),
        P("gx", "gy"),
        P("gx", "gy"),
    )
    out_specs = (P("gx", "gy"), P("gx", "gy"))
    return jax.shard_map(
        on_device, mesh=mesh, in_specs=in_specs, out_specs=out_specs, check_vma=False
    )
```

time: 93.7 us -> 88.2 us (0.941); the launches traced: 92.6 us -> 88 us
  local copies, waits for them, and re-layouts: 7.35 us -> 3.02 us
    unnamed x16 -> x2, local copies, waits for them, and re-layouts: 7.35 us -> 3.02 us
where the time goes in v2:
time: 88.2 us; the launch traced here: 88 us
  Pallas kernels  84.4 us (96%)
  local copies, waits for them, and re-layouts  3.02 us (3%)
    pallas_call x1, Pallas kernels, on_device(): pl.pallas_call(layer_kernel, name='decoder_layer', out_shape=(jax.ShapeDt...  84.4 us
    unnamed x2, local copies, waits for them, and re-layouts  3.02 us

profile of v2, /device:TPU:1, one launch (start us, length us, event | category | flops | bytes accessed | tf_op | source)
XLA Modules:
  0.0 88.0 jit_solution(2201247508585836744)
XLA Ops:
  0.6 84.4 %decoder_layer.1 = (bf16[96,256]{1,0:T(8,128)(2,1)}, bf16[96,896]{1,0:T(8,128)(2,1)}) custom-call(s32[192]{0:T(256)} %len_hbm.1, bf16[192,4,8,128]{3,2,1,0:T(8,128)(2,1)} %q_hbm.1, bf16[6,1,2048,128]{3,2,1,0:T(8,128)(2,1)} %k_hbm.1, bf16[6,1,2048,128]{3,2,1,0:T(8,128)(2,1)} %v_hbm.1, bf16[6,4,128]{2,1,0:T(4,128)(2,1)} %bitcast.4, ...), custom_call_target="tpu_custom_call" | custom-call | tf_op jit(solution)/shard_map/decoder_layer/pallas_call | solution.py:622
  85.0 1.4 %copy.15 = bf16[96,256]{1,0:T(8,128)(2,1)} copy(bf16[96,256]{1,0:T(8,128)(2,1)} %get-tuple-element.4) | data formatting | bytes 98304
  86.4 1.6 %copy.16 = bf16[96,896]{1,0:T(8,128)(2,1)} copy(bf16[96,896]{1,0:T(8,128)(2,1)} %get-tuple-element.5) | data formatting | bytes 344064

commit v3 on v2

--- a/solution.py
+++ b/solution.py
@@ -30,8 +30,8 @@
 BASE = (0,)
 PARTS = len(PER)
 SPLIT = ((80, 16),)
-LAG = 2
-LAG2 = 5
+LAG = 1
+LAG2 = 3
 STEP = 2
 
 

time: 88.2 us -> 87 us (0.986)
  Pallas kernels: 84.4 us -> 83.1 us
    pallas_call x1, Pallas kernels: 84.4 us -> 83.1 us  [on_device(): pl.pallas_call(layer_kernel, name='decoder_layer', out_shape=(jax.ShapeDt...]
where the time goes in v3:
time: 87 us; the launch traced here: 86.8 us
  Pallas kernels  83.1 us (96%)
  local copies, waits for them, and re-layouts  3.02 us (3%)
    pallas_call x1, Pallas kernels, on_device(): pl.pallas_call(layer_kernel, name='decoder_layer', out_shape=(jax.ShapeDt...  83.1 us
    unnamed x2, local copies, waits for them, and re-layouts  3.02 us

profile of v3, /device:TPU:1, one launch (start us, length us, event | category | flops | bytes accessed | tf_op | source)
XLA Modules:
  0.0 86.8 jit_solution(2442310250402114175)
XLA Ops:
  0.6 83.1 %decoder_layer.1 = (bf16[96,256]{1,0:T(8,128)(2,1)}, bf16[96,896]{1,0:T(8,128)(2,1)}) custom-call(s32[192]{0:T(256)} %len_hbm.1, bf16[192,4,8,128]{3,2,1,0:T(8,128)(2,1)} %q_hbm.1, bf16[6,1,2048,128]{3,2,1,0:T(8,128)(2,1)} %k_hbm.1, bf16[6,1,2048,128]{3,2,1,0:T(8,128)(2,1)} %v_hbm.1, bf16[6,4,128]{2,1,0:T(4,128)(2,1)} %bitcast.4, ...), custom_call_target="tpu_custom_call" | custom-call | tf_op jit(solution)/shard_map/decoder_layer/pallas_call | solution.py:622
  83.8 1.4 %copy.15 = bf16[96,256]{1,0:T(8,128)(2,1)} copy(bf16[96,256]{1,0:T(8,128)(2,1)} %get-tuple-element.4) | data formatting | bytes 98304
  85.2 1.6 %copy.16 = bf16[96,896]{1,0:T(8,128)(2,1)} copy(bf16[96,896]{1,0:T(8,128)(2,1)} %get-tuple-element.5) | data formatting | bytes 344064

commit v4 on v3

--- a/solution.py
+++ b/solution.py
@@ -508,10 +508,13 @@
                 x_other[rows, cols] = g2[yy, 4 * (1 - c) + m, part_of(h)]
                 x_own[rows, cols] = g2[yy, 4 * c + m, part_of(h)]
 
-        def multiply(j):
+        def multiply_other(j, carry):
             other = jnp.dot(x_other[core_rows(h), :], w_v[j], preferred_element_type=F32)
             cp_s[j, core_rows(h)] = other.astype(BF16)
             cp_copy(h, j).start()
+            return carry
+
+        def multiply(j):
             own[j, core_rows(h)] = jnp.dot(
                 x_own[core_rows(h), :], w_v[j], preferred_element_type=F32
             )
@@ -548,6 +551,7 @@
 
             return carry
 
+        lax.fori_loop(0, CHUNKS, multiply_other, 0)
         lax.fori_loop(0, CHUNKS + LAG2, step, 0)
 
         def close_chunks():

time: 87 us -> 87.9 us (1.010)
  Pallas kernels: 83.1 us -> 84.1 us
    pallas_call x1, Pallas kernels: 83.1 us -> 84.1 us  [on_device(): pl.pallas_call(layer_kernel, name='decoder_layer', out_shape=(jax.ShapeDt...]
where the time goes in v4:
time: 87.9 us; the launch traced here: 87.8 us
  Pallas kernels  84.1 us (96%)
  local copies, waits for them, and re-layouts  3.02 us (3%)
    pallas_call x1, Pallas kernels, on_device(): pl.pallas_call(layer_kernel, name='decoder_layer', out_shape=(jax.ShapeDt...  84.1 us
    unnamed x2, local copies, waits for them, and re-layouts  3.02 us

profile of v4, /device:TPU:1, one launch (start us, length us, event | category | flops | bytes accessed | tf_op | source)
XLA Modules:
  0.0 87.8 jit_solution(15501409758436166930)
XLA Ops:
  0.6 84.1 %decoder_layer.1 = (bf16[96,256]{1,0:T(8,128)(2,1)}, bf16[96,896]{1,0:T(8,128)(2,1)}) custom-call(s32[192]{0:T(256)} %len_hbm.1, bf16[192,4,8,128]{3,2,1,0:T(8,128)(2,1)} %q_hbm.1, bf16[6,1,2048,128]{3,2,1,0:T(8,128)(2,1)} %k_hbm.1, bf16[6,1,2048,128]{3,2,1,0:T(8,128)(2,1)} %v_hbm.1, bf16[6,4,128]{2,1,0:T(4,128)(2,1)} %bitcast.4, ...), custom_call_target="tpu_custom_call" | custom-call | tf_op jit(solution)/shard_map/decoder_layer/pallas_call | solution.py:626
  84.7 1.4 %copy.15 = bf16[96,256]{1,0:T(8,128)(2,1)} copy(bf16[96,256]{1,0:T(8,128)(2,1)} %get-tuple-element.4) | data formatting | bytes 98304
  86.2 1.6 %copy.16 = bf16[96,896]{1,0:T(8,128)(2,1)} copy(bf16[96,896]{1,0:T(8,128)(2,1)} %get-tuple-element.5) | data formatting | bytes 344064
